TPU v7x, 32 devices: a whole 2x2x4 slice. The times are simulated.
32 devices in a mesh: gx: 4 (over x, core), gy: 4 (over z), gz: 2 (over y).
Axes of the slice: x: 2, y: 2, z: 4, core: 2. Of those that a mesh axis runs over, the one named last changes fastest.
Arguments:
- field: float32 [2, 32, 256, 512], P(None, 'gz', 'gx', 'gy'), may hold values from -30 to 30
- transfer: float32 [4, 128], replicated, may hold values from 0.2 to 3
- light_angles: float32 [2], replicated, may hold values from -3.140625 to 3.140625
Outputs:
- image: float32 [4, 256, 512], P(None, ('gx', 'gz'), 'gy')
All inputs are finite; a program needn't handle non-finite values.
Results may differ from a plain program's by a relative error of at most 0.00019.
Values sent between devices are 32-bit elements; how exact they have to be, the bound alone decides.
A program may use at most 64 MiB of HBM per device.

v0:
```python
import math

import jax
import jax.numpy as jnp
from jax import lax
from jax.sharding import PartitionSpec as P

SIGMA_TAPS = 1.2
OPTICAL = 2.0
SHADE_FLOOR = 0.25


def extended(value, sides, width):
    for axis, dim in sides:
        size, length = (lax.axis_size(axis), value.shape[dim])
        up = [(i, (i + 1) % size) for i in range(size - 1)]
        down = [(j, i) for i, j in up]
        last = lax.slice_in_dim(value, length - width, length, axis=dim)
        initial = lax.slice_in_dim(value, 0, width, axis=dim)
        before = lax.ppermute(last, axis, up)
        after = lax.ppermute(initial, axis, down)
        value = jnp.concatenate([before, value, after], axis=dim)
    return value


def carried_in(value, axis, combine, identity, reverse):
    length, here = (lax.axis_size(axis), lax.axis_index(axis))
    everything = lax.all_gather(value, axis)
    start = jnp.broadcast_to(jnp.asarray(identity, value.dtype), value.shape)

    def turn(k, before):
        at = length - 1 - k if reverse else k
        reached = at > here if reverse else at < here
        new = combine(before, everything[at])
        return jnp.where(reached, new, before)

    return lax.fori_loop(0, length, turn, start)


def filter_taps():
    places = [-3, -2, -1, 0, 1, 2, 3]
    bell = [math.exp(-place * place / (2.0 * SIGMA_TAPS * SIGMA_TAPS)) for place in places]
    bell_total = sum(bell)
    slope_total = sum((place * place * weight for place, weight in zip(places, bell)))
    smooth_taps = [weight / bell_total for weight in bell]
    slope_taps = [place * weight / slope_total for place, weight in zip(places, bell)]
    return (smooth_taps, slope_taps)


def sweep(volume, taps, axis_dim):
    length = volume.shape[axis_dim] - 6
    total = taps[0] * lax.slice_in_dim(volume, 0, length, axis=axis_dim)
    for place in range(1, 7):
        total = total + taps[place] * lax.slice_in_dim(volume, place, place + length, axis=axis_dim)
    return total


def depth_section(first, second):
    smooth_taps, slope_taps = filter_taps()
    return (
        sweep(first, smooth_taps, 0),
        sweep(first, slope_taps, 0),
        sweep(second, smooth_taps, 0),
    )


def cross_section(plain, slope, other):
    smooth_taps, slope_taps = filter_taps()
    return (
        sweep(plain, smooth_taps, 1),
        sweep(plain, slope_taps, 1),
        sweep(slope, smooth_taps, 1),
        sweep(other, smooth_taps, 1),
    )


def row_section(plain, cross_slope, depth_slope, other):
    smooth_taps, slope_taps = filter_taps()
    value = sweep(plain, smooth_taps, 2)
    grad_y = sweep(plain, slope_taps, 2)
    grad_x = sweep(cross_slope, smooth_taps, 2)
    grad_z = sweep(depth_slope, smooth_taps, 2)
    mixture = sweep(other, smooth_taps, 2)
    return (value, mixture, grad_x, grad_y, grad_z)


def sample_plane(value, mixture, grad_x, grad_y, grad_z, transfer, light_angles, depth_step):
    bins = transfer.shape[1]
    position = jax.nn.sigmoid(value) * (bins - 1)
    centers = jnp.arange(bins).astype(position.dtype)
    tent = jnp.maximum(0.0, 1.0 - jnp.abs(position[None] - centers[:, None, None]))
    looked = jnp.einsum("cb,bxy->cxy", transfer, tent, precision=lax.Precision.HIGHEST)
    light_x = jnp.cos(light_angles[0]) * jnp.sin(light_angles[1])
    light_y = jnp.sin(light_angles[0]) * jnp.sin(light_angles[1])
    light_z = jnp.cos(light_angles[1])
    facing = grad_x * light_x + grad_y * light_y + grad_z * light_z
    diffuse = facing * facing / (grad_x * grad_x + grad_y * grad_y + grad_z * grad_z + SHADE_FLOOR)
    shade = 0.25 + 0.75 * diffuse
    alpha = 1.0 - jnp.exp(-OPTICAL * looked[3] * jax.nn.sigmoid(mixture) * depth_step)
    return jnp.concatenate([(alpha * shade)[None] * looked[:3], alpha[None]], 0)


def over(front, back):
    return front + (1.0 - front[3:4]) * back


def over_reversed(later_back, nearer):
    return over(nearer, later_back)


def integrate(value, mixture, grad_x, grad_y, grad_z, transfer, light_angles, depth_step):

    def advance(running, planes):
        sample = sample_plane(
            planes[0],
            planes[1],
            planes[2],
            planes[3],
            planes[4],
            transfer,
            light_angles,
            depth_step,
        )
        return (over(running, sample), None)

    start = jnp.zeros((4,) + value.shape[1:], value.dtype)
    result, unused = lax.scan(advance, start, (value, mixture, grad_x, grad_y, grad_z))
    return result


def shards(field, transfer, light_angles):
    depth_count = lax.axis_size("gz")
    depth_step = 1.0 / (field.shape[1] * depth_count)
    padded = extended(field, (("gx", 2), ("gy", 3), ("gz", 1)), 3)
    plain, slope, other = depth_section(padded[0], padded[1])
    cross_plain, cross_slope, depth_slope, cross_other = cross_section(plain, slope, other)
    value, mixture, grad_x, grad_y, grad_z = row_section(
        cross_plain, cross_slope, depth_slope, cross_other
    )
    partial_value = integrate(
        value, mixture, grad_x, grad_y, grad_z, transfer, light_angles, depth_step
    )
    empty = jnp.zeros_like(partial_value)
    in_front = carried_in(partial_value, "gz", over, empty, False)
    behind = carried_in(partial_value, "gz", over_reversed, empty, True)
    whole = over(over(in_front, partial_value), behind)
    row_count = partial_value.shape[1] // depth_count
    return lax.dynamic_slice_in_dim(whole, lax.axis_index("gz") * row_count, row_count, 1)


def solution(mesh):
    placed = (P(None, "gz", "gx", "gy"), P(), P())
    return jax.shard_map(
        shards, mesh=mesh, in_specs=placed, out_specs=P(None, ("gx", "gz"), "gy"), check_vma=False
    )
```

profile of v0, /device:TPU:0, one launch (start us, length us, event | category | flops | bytes accessed | tf_op | source)
XLA Modules:
  0.0 149.5 jit_solution(15889656817000057151)
XLA Ops:
  0.0 1.0 fusion.61
  1.0 2.4 %collective-permute-start = (f32[2,16,3,128]{3,1,2,0:T(8,128)S(1)}, f32[2,16,3,128]{3,1,2,0:T(8,128)S(1)}, u32[]{:S(2)}, u32[]{:S(2)}) collective-permute-start(f32[2,16,3,128]{3,1,2,0:T(8,128)S(1)} %copy.54), channel_id=1, source_target_pairs={{0,8},{8,16},{16,24},{1,9},{9,17},{17,25},{2,10},{10,18},{18,26},{... | collective-permute-start | bytes 147464 | tf_op jit(solution)/shard_map/ppermute | solution.py:20
  3.4 1.3 collective-permute-start.1
  4.7 2.2 %copy.43 = f32[2,16,64,128]{2,1,3,0:T(8,128)S(1)} copy(f32[2,16,64,128]{3,2,1,0:T(8,128)} %param.9) | data formatting | bytes 2097152 | tf_op args[0]
  6.9 2.1 %copy.42 = f32[2,16,3,128]{2,1,3,0:T(8,128)} copy(f32[2,16,3,128]{3,1,2,0:T(8,128)S(1)} %collective-permute-done) | data formatting | bytes 98304 | tf_op jit(solution)/shard_map/ppermute | solution.py:20
  9.0 2.1 %copy.44 = f32[2,16,3,128]{2,1,3,0:T(8,128)} copy(f32[2,16,3,128]{3,1,2,0:T(8,128)S(1)} %collective-permute-done.1) | data formatting | bytes 98304 | tf_op jit(solution)/shard_map/ppermute | solution.py:21
  11.1 1.1 pad_maximum_fusion.4
  12.2 4.4 %collective-permute-start.2 = (f32[2,16,70,3]{2,1,3,0:T(8,128)S(1)}, f32[2,16,70,3]{2,1,3,0:T(8,128)S(1)}, u32[]{:S(2)}, u32[]{:S(2)}) collective-permute-start(f32[2,16,70,3]{2,1,3,0:T(8,128)S(1)} %get-tuple-element.458), channel_id=1, source_target_pairs={{0,2},{2,4},{4,6},{1,3},{3,5},{5,7},{8,10},{10,12},{12,14},{9,11},... | collective-permute-start | bytes 80648 | tf_op jit(solution)/shard_map/ppermute | solution.py:20
  16.7 1.3 collective-permute-start.3
  18.4 4.3 %collective-permute-done.3 = f32[2,16,70,3]{2,1,3,0:T(8,128)S(1)} collective-permute-done((f32[2,16,70,3]{2,1,3,0:T(8,128)S(1)}, f32[2,16,70,3]{2,1,3,0:T(8,128)S(1)}, u32[]{:S(2)}, u32[]{:S(2)}) %collective-permute-start.3) | collective-permute-done | bytes 26912 | tf_op jit(solution)/shard_map/ppermute | solution.py:21
  22.7 1.1 pad_maximum_fusion.1
  24.0 1.2 copy-done.2
  25.4 3.4 %collective-permute-start.4 = (f32[2,3,70,134]{2,0,3,1:T(2,128)S(1)}, f32[2,3,70,134]{2,0,3,1:T(2,128)S(1)}, u32[]{:S(2)}, u32[]{:S(2)}) collective-permute-start(f32[2,3,70,134]{2,0,3,1:T(2,128)S(1)} %copy.45), channel_id=1, source_target_pairs={{0,1},{2,3},{4,5},{6,7},{8,9},{10,11},{12,13},{14,15},{16,17},{18,... | collective-permute-start | bytes 675368 | tf_op jit(solution)/shard_map/ppermute | solution.py:20
  28.9 1.0 copy.47
  29.9 1.3 collective-permute-start.5
  34.6 4.1 %collective-permute-done.4 = f32[2,3,70,134]{2,0,3,1:T(2,128)S(1)} collective-permute-done((f32[2,3,70,134]{2,0,3,1:T(2,128)S(1)}, f32[2,3,70,134]{2,0,3,1:T(2,128)S(1)}, u32[]{:S(2)}, u32[]{:S(2)}) %collective-permute-start.4) | collective-permute-done | bytes 225152 | tf_op jit(solution)/shard_map/ppermute | solution.py:20
  38.9 5.3 %collective-permute-done.5 = f32[2,3,70,134]{2,0,3,1:T(2,128)} collective-permute-done((f32[2,3,70,134]{2,0,3,1:T(2,128)}, f32[2,3,70,134]{2,0,3,1:T(2,128)}, u32[]{:S(2)}, u32[]{:S(2)}) %collective-permute-start.5) | collective-permute-done | bytes 225152 | tf_op jit(solution)/shard_map/ppermute | solution.py:21
  44.2 1.1 copy.48
  45.3 6.8 %maximum_maximum_fusion = (f32[2,19,70,134]{2,1,3,0:T(8,128)S(1)}, f32[2,19,70,134]{2,1,3,0:T(8,128)S(1)}) fusion(f32[2,16,70,3]{2,1,3,0:T(8,128)S(1)} %collective-permute-done.3, f32[2,16,3,128]{2,1,3,0:T(8,128)} %copy.44, f32[2,16,64,128]{2,1,3,0:T(8,128)S(1)} %copy.43, f32[2,16,3,128]{2,1,3,0:T(8,128)} %copy.42, ...), kind=kLoop, calls=%fused_computation.36 | loop fusion | flops 3564400 | bytes 4502400 | tf_op jit(solution)/shard_map/concatenate | solution.py:22
  52.1 0.8 fusion.34
  53.0 1.3 add_bitcast_fusion
  54.3 1.8 %fusion.27 = f32[16,64,134]{1,0,2:T(8,128)S(1)} fusion(f32[16,70,134]{1,0,2:T(8,128)S(1)} %fusion.34), kind=kLoop, calls=%fused_computation.53 | loop fusion | flops 1783808 | bytes 4390912 | tf_op jit(solution)/shard_map/add | solution.py:54
  56.4 1.2 copy.50
  57.6 1.8 %multiply_add_fusion = (f32[16,64,134]{1,0,2:T(8,128)S(1)}, f32[16,64,134]{1,0,2:T(8,128)S(1)}) fusion(f32[16,70,134]{1,0,2:T(8,128)S(1)} %get-tuple-element.455), kind=kLoop, calls=%fused_computation.81 | loop fusion | flops 3567616 | bytes 4939776 | tf_op jit(solution)/shard_map/add | solution.py:54
  59.4 1.8 %multiply_add_fusion.2 = (f32[16,64,128]{1,0,2:T(8,128)S(1)}, f32[16,64,128]{1,0,2:T(8,128)}) fusion(f32[16,64,134]{1,0,2:T(8,128)S(1)} %get-tuple-element.465), kind=kLoop, calls=%fused_computation.122 | loop fusion | flops 3407872 | bytes 4718592 | tf_op jit(solution)/shard_map/add | solution.py:54
  61.1 2.4 %copy.49 = f32[16,64,128]{2,1,0:T(8,128)} copy(f32[16,64,128]{1,0,2:T(8,128)} %get-tuple-element.463) | data formatting | bytes 1048576
  63.6 1.2 copy.52
  65.6 1.8 %fusion.21 = f32[16,64,134]{1,0,2:T(8,128)S(1)} fusion(f32[16,70,134]{1,0,2:T(8,128)S(1)} %get-tuple-element.454), kind=kLoop, calls=%fused_computation.40 | loop fusion | flops 1783808 | bytes 4390912 | tf_op jit(solution)/shard_map/add | solution.py:54
  68.4 73.5 %while.43 = (s32[]{:T(128)}, f32[4,64,128]{2,1,0:T(8,128)S(1)}, f32[16,64,128]{2,1,0:T(8,128)}, f32[4,128]{1,0:T(4,128)S(1)}, f32[16,64,128]{2,1,0:T(8,128)}, /*...) while((s32[]{:T(128)}, f32[4,64,128]{2,1,0:T(8,128)S(1)}, ...), condition=%wide.region_1.2_spmd.clone, body=%wide.region_0.1_spmd.clone.sunk | while | flops 54943872 | bytes 1707164 | solution.py:127
  69.2 2.8 %fusion.73 = f32[64,128,4]{1,2,0:T(4,128)S(1)} fusion(f32[128]{0:T(128)S(1)} %iota_convert_fusion.2, f32[64,128]{1,0:T(8,128)S(1)} %multiply_bitcast_fusion.4, f32[4,128]{1,0:T(4,128)S(1)} %get-tuple-element.620), kind=kOutput, calls=%fused_computation.clone.1 | convolution fusion | flops 54525952 | bytes 166400 | tf_op jit(solution)/shard_map/while/body/eval_jaxpr/cb,bxy->cxy/dot_general | solution.py:92
  72.0 0.8 multiply_bitcast_fusion.5
  73.7 2.8 %fusion.73 = f32[64,128,4]{1,2,0:T(4,128)S(1)} fusion(f32[128]{0:T(128)S(1)} %iota_convert_fusion.2, f32[64,128]{1,0:T(8,128)S(1)} %multiply_bitcast_fusion.4, f32[4,128]{1,0:T(4,128)S(1)} %get-tuple-element.620), kind=kOutput, calls=%fused_computation.clone.1 | convolution fusion | flops 54525952 | bytes 166400 | tf_op jit(solution)/shard_map/while/body/eval_jaxpr/cb,bxy->cxy/dot_general | solution.py:92
  76.6 0.8 multiply_bitcast_fusion.5
  77.5 0.8 multiply_bitcast_fusion.4
  78.3 2.8 %fusion.73 = f32[64,128,4]{1,2,0:T(4,128)S(1)} fusion(f32[128]{0:T(128)S(1)} %iota_convert_fusion.2, f32[64,128]{1,0:T(8,128)S(1)} %multiply_bitcast_fusion.4, f32[4,128]{1,0:T(4,128)S(1)} %get-tuple-element.620), kind=kOutput, calls=%fused_computation.clone.1 | convolution fusion | flops 54525952 | bytes 166400 | tf_op jit(solution)/shard_map/while/body/eval_jaxpr/cb,bxy->cxy/dot_general | solution.py:92
  81.2 0.8 multiply_bitcast_fusion.5
  82.1 0.8 multiply_bitcast_fusion.4
  82.9 2.8 %fusion.73 = f32[64,128,4]{1,2,0:T(4,128)S(1)} fusion(f32[128]{0:T(128)S(1)} %iota_convert_fusion.2, f32[64,128]{1,0:T(8,128)S(1)} %multiply_bitcast_fusion.4, f32[4,128]{1,0:T(4,128)S(1)} %get-tuple-element.620), kind=kOutput, calls=%fused_computation.clone.1 | convolution fusion | flops 54525952 | bytes 166400 | tf_op jit(solution)/shard_map/while/body/eval_jaxpr/cb,bxy->cxy/dot_general | solution.py:92
  85.8 0.8 multiply_bitcast_fusion.5
  87.5 2.8 %fusion.73 = f32[64,128,4]{1,2,0:T(4,128)S(1)} fusion(f32[128]{0:T(128)S(1)} %iota_convert_fusion.2, f32[64,128]{1,0:T(8,128)S(1)} %multiply_bitcast_fusion.4, f32[4,128]{1,0:T(4,128)S(1)} %get-tuple-element.620), kind=kOutput, calls=%fused_computation.clone.1 | convolution fusion | flops 54525952 | bytes 166400 | tf_op jit(solution)/shard_map/while/body/eval_jaxpr/cb,bxy->cxy/dot_general | solution.py:92
  90.4 0.8 multiply_bitcast_fusion.5
  92.1 2.8 %fusion.73 = f32[64,128,4]{1,2,0:T(4,128)S(1)} fusion(f32[128]{0:T(128)S(1)} %iota_convert_fusion.2, f32[64,128]{1,0:T(8,128)S(1)} %multiply_bitcast_fusion.4, f32[4,128]{1,0:T(4,128)S(1)} %get-tuple-element.620), kind=kOutput, calls=%fused_computation.clone.1 | convolution fusion | flops 54525952 | bytes 166400 | tf_op jit(solution)/shard_map/while/body/eval_jaxpr/cb,bxy->cxy/dot_general | solution.py:92
  95.0 0.8 multiply_bitcast_fusion.5
  96.7 2.8 %fusion.73 = f32[64,128,4]{1,2,0:T(4,128)S(1)} fusion(f32[128]{0:T(128)S(1)} %iota_convert_fusion.2, f32[64,128]{1,0:T(8,128)S(1)} %multiply_bitcast_fusion.4, f32[4,128]{1,0:T(4,128)S(1)} %get-tuple-element.620), kind=kOutput, calls=%fused_computation.clone.1 | convolution fusion | flops 54525952 | bytes 166400 | tf_op jit(solution)/shard_map/while/body/eval_jaxpr/cb,bxy->cxy/dot_general | solution.py:92
  99.6 0.8 multiply_bitcast_fusion.5
  101.3 2.8 %fusion.73 = f32[64,128,4]{1,2,0:T(4,128)S(1)} fusion(f32[128]{0:T(128)S(1)} %iota_convert_fusion.2, f32[64,128]{1,0:T(8,128)S(1)} %multiply_bitcast_fusion.4, f32[4,128]{1,0:T(4,128)S(1)} %get-tuple-element.620), kind=kOutput, calls=%fused_computation.clone.1 | convolution fusion | flops 54525952 | bytes 166400 | tf_op jit(solution)/shard_map/while/body/eval_jaxpr/cb,bxy->cxy/dot_general | solution.py:92
  104.1 0.8 multiply_bitcast_fusion.5
  105.9 2.8 %fusion.73 = f32[64,128,4]{1,2,0:T(4,128)S(1)} fusion(f32[128]{0:T(128)S(1)} %iota_convert_fusion.2, f32[64,128]{1,0:T(8,128)S(1)} %multiply_bitcast_fusion.4, f32[4,128]{1,0:T(4,128)S(1)} %get-tuple-element.620), kind=kOutput, calls=%fused_computation.clone.1 | convolution fusion | flops 54525952 | bytes 166400 | tf_op jit(solution)/shard_map/while/body/eval_jaxpr/cb,bxy->cxy/dot_general | solution.py:92
  108.7 0.8 multiply_bitcast_fusion.5
  110.5 2.8 %fusion.73 = f32[64,128,4]{1,2,0:T(4,128)S(1)} fusion(f32[128]{0:T(128)S(1)} %iota_convert_fusion.2, f32[64,128]{1,0:T(8,128)S(1)} %multiply_bitcast_fusion.4, f32[4,128]{1,0:T(4,128)S(1)} %get-tuple-element.620), kind=kOutput, calls=%fused_computation.clone.1 | convolution fusion | flops 54525952 | bytes 166400 | tf_op jit(solution)/shard_map/while/body/eval_jaxpr/cb,bxy->cxy/dot_general | solution.py:92
  113.3 0.8 multiply_bitcast_fusion.5
  115.1 2.8 %fusion.73 = f32[64,128,4]{1,2,0:T(4,128)S(1)} fusion(f32[128]{0:T(128)S(1)} %iota_convert_fusion.2, f32[64,128]{1,0:T(8,128)S(1)} %multiply_bitcast_fusion.4, f32[4,128]{1,0:T(4,128)S(1)} %get-tuple-element.620), kind=kOutput, calls=%fused_computation.clone.1 | convolution fusion | flops 54525952 | bytes 166400 | tf_op jit(solution)/shard_map/while/body/eval_jaxpr/cb,bxy->cxy/dot_general | solution.py:92
  117.9 0.8 multiply_bitcast_fusion.5
  119.7 2.8 %fusion.73 = f32[64,128,4]{1,2,0:T(4,128)S(1)} fusion(f32[128]{0:T(128)S(1)} %iota_convert_fusion.2, f32[64,128]{1,0:T(8,128)S(1)} %multiply_bitcast_fusion.4, f32[4,128]{1,0:T(4,128)S(1)} %get-tuple-element.620), kind=kOutput, calls=%fused_computation.clone.1 | convolution fusion | flops 54525952 | bytes 166400 | tf_op jit(solution)/shard_map/while/body/eval_jaxpr/cb,bxy->cxy/dot_general | solution.py:92
  122.5 0.8 multiply_bitcast_fusion.5
  124.3 2.8 %fusion.73 = f32[64,128,4]{1,2,0:T(4,128)S(1)} fusion(f32[128]{0:T(128)S(1)} %iota_convert_fusion.2, f32[64,128]{1,0:T(8,128)S(1)} %multiply_bitcast_fusion.4, f32[4,128]{1,0:T(4,128)S(1)} %get-tuple-element.620), kind=kOutput, calls=%fused_computation.clone.1 | convolution fusion | flops 54525952 | bytes 166400 | tf_op jit(solution)/shard_map/while/body/eval_jaxpr/cb,bxy->cxy/dot_general | solution.py:92
  127.1 0.8 multiply_bitcast_fusion.5
  128.9 2.8 %fusion.73 = f32[64,128,4]{1,2,0:T(4,128)S(1)} fusion(f32[128]{0:T(128)S(1)} %iota_convert_fusion.2, f32[64,128]{1,0:T(8,128)S(1)} %multiply_bitcast_fusion.4, f32[4,128]{1,0:T(4,128)S(1)} %get-tuple-element.620), kind=kOutput, calls=%fused_computation.clone.1 | convolution fusion | flops 54525952 | bytes 166400 | tf_op jit(solution)/shard_map/while/body/eval_jaxpr/cb,bxy->cxy/dot_general | solution.py:92
  131.7 0.8 multiply_bitcast_fusion.5
  133.4 2.8 %fusion.73 = f32[64,128,4]{1,2,0:T(4,128)S(1)} fusion(f32[128]{0:T(128)S(1)} %iota_convert_fusion.2, f32[64,128]{1,0:T(8,128)S(1)} %multiply_bitcast_fusion.4, f32[4,128]{1,0:T(4,128)S(1)} %get-tuple-element.620), kind=kOutput, calls=%fused_computation.clone.1 | convolution fusion | flops 54525952 | bytes 166400 | tf_op jit(solution)/shard_map/while/body/eval_jaxpr/cb,bxy->cxy/dot_general | solution.py:92
  136.3 0.8 multiply_bitcast_fusion.5
  138.0 2.8 %fusion.73 = f32[64,128,4]{1,2,0:T(4,128)S(1)} fusion(f32[128]{0:T(128)S(1)} %iota_convert_fusion.2, f32[64,128]{1,0:T(8,128)S(1)} %multiply_bitcast_fusion.4, f32[4,128]{1,0:T(4,128)S(1)} %get-tuple-element.620), kind=kOutput, calls=%fused_computation.clone.1 | convolution fusion | flops 54525952 | bytes 166400 | tf_op jit(solution)/shard_map/while/body/eval_jaxpr/cb,bxy->cxy/dot_general | solution.py:92
  140.9 0.8 multiply_bitcast_fusion.5
  141.8 5.9 %all-gather = f32[8,64,128]{2,1,0:T(8,128)S(1)} all-gather(f32[4,64,128]{2,1,0:T(8,128)S(1)} %get-tuple-element.312), channel_id=2, replica_groups=mesh['gx'=4,'gy'=4,'gz'=2] {'gz'}, dimensions={0}, use_global_device_ids=true | all-gather | bytes 393216 | tf_op jit(solution)/shard_map/all_gather | solution.py:28
  (157 shorter events, 18.1 us)
Async XLA Ops:
  1.0 5.8 %collective-permute-start = (f32[2,16,3,128]{3,1,2,0:T(8,128)S(1)}, f32[2,16,3,128]{3,1,2,0:T(8,128)S(1)}, u32[]{:S(2)}, u32[]{:S(2)}) collective-permute-start(f32[2,16,3,128]{3,1,2,0:T(8,128)S(1)} %copy.54), channel_id=1, source_target_pairs={{0,8},{8,16},{16,24},{1,9},{9,17},{17,25},{2,10},{10,18},{18,26},{... | collective-permute-start | bytes 147464 | tf_op jit(solution)/shard_map/ppermute | solution.py:20
  3.4 5.6 %collective-permute-start.1 = (f32[2,16,3,128]{3,1,2,0:T(8,128)S(1)}, f32[2,16,3,128]{3,1,2,0:T(8,128)S(1)}, u32[]{:S(2)}, u32[]{:S(2)}) collective-permute-start(f32[2,16,3,128]{3,1,2,0:T(8,128)S(1)} %copy.55), channel_id=1, source_target_pairs={{8,0},{16,8},{24,16},{9,1},{17,9},{25,17},{10,2},{18,10},{26,18},{... | collective-permute-start | bytes 147464 | tf_op jit(solution)/shard_map/ppermute | solution.py:21
  11.1 11.6 %copy-start = (f32[2,16,3,128]{2,1,3,0:T(8,128)S(1)}, f32[2,16,3,128]{2,1,3,0:T(8,128)}, u32[]{:S(2)}) copy-start(f32[2,16,3,128]{2,1,3,0:T(8,128)} %copy.42) | copy-start | bytes 147460
  11.1 11.6 %copy-start.1 = (f32[2,16,3,128]{2,1,3,0:T(8,128)S(1)}, f32[2,16,3,128]{2,1,3,0:T(8,128)}, u32[]{:S(2)}) copy-start(f32[2,16,3,128]{2,1,3,0:T(8,128)} %copy.44) | copy-start | bytes 147460
  12.2 6.2 %collective-permute-start.2 = (f32[2,16,70,3]{2,1,3,0:T(8,128)S(1)}, f32[2,16,70,3]{2,1,3,0:T(8,128)S(1)}, u32[]{:S(2)}, u32[]{:S(2)}) collective-permute-start(f32[2,16,70,3]{2,1,3,0:T(8,128)S(1)} %get-tuple-element.458), channel_id=1, source_target_pairs={{0,2},{2,4},{4,6},{1,3},{3,5},{5,7},{8,10},{10,12},{12,14},{9,11},... | collective-permute-start | bytes 80648 | tf_op jit(solution)/shard_map/ppermute | solution.py:20
  16.7 6.0 %collective-permute-start.3 = (f32[2,16,70,3]{2,1,3,0:T(8,128)S(1)}, f32[2,16,70,3]{2,1,3,0:T(8,128)S(1)}, u32[]{:S(2)}, u32[]{:S(2)}) collective-permute-start(f32[2,16,70,3]{2,1,3,0:T(8,128)S(1)} %get-tuple-element.459), channel_id=1, source_target_pairs={{2,0},{4,2},{6,4},{3,1},{5,3},{7,5},{10,8},{12,10},{14,12},{11,9},... | collective-permute-start | bytes 80648 | tf_op jit(solution)/shard_map/ppermute | solution.py:21
  23.8 1.4 copy-start.2
  25.2 5.9 %copy-start.5 = (f32[2]{0:T(128)S(1)}, f32[2]{0:T(128)}, u32[]{:S(2)}) copy-start(f32[2]{0:T(128)} %param.11) | copy-start | bytes 28
  25.4 13.3 %collective-permute-start.4 = (f32[2,3,70,134]{2,0,3,1:T(2,128)S(1)}, f32[2,3,70,134]{2,0,3,1:T(2,128)S(1)}, u32[]{:S(2)}, u32[]{:S(2)}) collective-permute-start(f32[2,3,70,134]{2,0,3,1:T(2,128)S(1)} %copy.45), channel_id=1, source_target_pairs={{0,1},{2,3},{4,5},{6,7},{8,9},{10,11},{12,13},{14,15},{16,17},{18,... | collective-permute-start | bytes 675368 | tf_op jit(solution)/shard_map/ppermute | solution.py:20
  29.9 14.3 %collective-permute-start.5 = (f32[2,3,70,134]{2,0,3,1:T(2,128)}, f32[2,3,70,134]{2,0,3,1:T(2,128)}, u32[]{:S(2)}, u32[]{:S(2)}) collective-permute-start(f32[2,3,70,134]{2,0,3,1:T(2,128)} %copy.47), channel_id=1, source_target_pairs={{1,0},{3,2},{5,4},{7,6},{9,8},{11,10},{13,12},{15,14},{17,16},{19,... | collective-permute-start | bytes 675368 | tf_op jit(solution)/shard_map/ppermute | solution.py:21
  45.3 6.8 %copy-start.3 = (f32[2,16,70,134]{2,1,3,0:T(8,128)S(1)}, f32[2,16,70,134]{2,1,3,0:T(8,128)}, u32[]{:S(2)}) copy-start(f32[2,16,70,134]{2,1,3,0:T(8,128)} %copy-done.2) | copy-start | bytes 3601924
  67.7 0.7 copy-start.6
  147.8 0.9 copy-start.4
where the time goes:
time: 152 us; the launch traced here: 150 us
  other arithmetic  47.2 us (31%)
  matrix products  45.2 us (30%)
  local copies, waits for them, and re-layouts  18.6 us (12%)
  starting transfers between devices  14.1 us (9%)
  waiting for transfers between devices  14.1 us (9%)
  blocking collectives  5.91 us (4%)
  between operations  3.13 us (2%)
    dot_general x16, matrix products, sample_plane(): jnp.einsum('cb,bxy->cxy', transfer, tent, precision=lax.Precision.HIGHEST)  45.2 us
    mul x32, other arithmetic, sample_plane(): return jnp.concatenate([(alpha * shade)[None] * looked[:3], alpha[None]], 0)  13.4 us
    sub x16, other arithmetic, sample_plane(): position[None] - centers[:, None, None]  12.5 us
    ppermute x3, starting transfers between devices, extended(): before = lax.ppermute(last, axis, up)  10.3 us
    add x9, other arithmetic, sweep(): total + taps[place] * lax.slice_in_dim(volume, place, place + length, axi...  10.2 us
    unnamed x22, local copies, waits for them, and re-layouts  9.98 us
    ppermute x3, waiting for transfers between devices, extended(): after = lax.ppermute(initial, axis, down)  9.53 us
    concatenate x2, other arithmetic, extended(): value = jnp.concatenate([before, value, after], axis=dim)  7.96 us
  transfers between devices with their start and end apart: 6, of which 4 were waited for; matrix products, arithmetic and copies ran while one was open for 4% of the time, Pallas kernels for 0%

commit v1 on v0

v1 whole, which is shorter than its diff:
```python
import functools
import math

import jax
import jax.numpy as jnp
from jax import lax
from jax.experimental import pallas as pl
from jax.experimental.pallas import tpu as pltpu
from jax.sharding import PartitionSpec as P

MESH = pl.DeviceIdType.MESH
SIGMA_TAPS = 1.2
OPTICAL = 2.0
SHADE_FLOOR = 0.25
EDGE = 8


def filter_taps():
    places = [-3, -2, -1, 0, 1, 2, 3]
    bell = [math.exp(-place * place / (2.0 * SIGMA_TAPS * SIGMA_TAPS)) for place in places]
    bell_total = sum(bell)
    slope_total = sum((place * place * weight for place, weight in zip(places, bell)))
    smooth_taps = [weight / bell_total for weight in bell]
    slope_taps = [place * weight / slope_total for place, weight in zip(places, bell)]
    return (smooth_taps, slope_taps)


def smooth_of(at):
    taps, _ = filter_taps()
    total = taps[3] * at(0)
    for o in (1, 2, 3):
        total = total + taps[3 + o] * (at(o) + at(-o))
    return total


def slope_of(at):
    _, taps = filter_taps()
    total = taps[4] * (at(1) - at(-1))
    for o in (2, 3):
        total = total + taps[3 + o] * (at(o) - at(-o))
    return total


def both_of(at):
    smooth, slope = filter_taps()
    plain, steep = smooth[3] * at(0), None
    for o in (1, 2, 3):
        after, before = at(o), at(-o)
        plain = plain + smooth[3 + o] * (after + before)
        term = slope[3 + o] * (after - before)
        steep = term if steep is None else steep + term
    return plain, steep


def kernel(sizes, depth_step, field, transfer, angles, out, box, own_strips, rim_strips, got_own, got_rim,
           rows_done, flat_done, table, light, inner, stage, slabs,
           local_sem, send_sem, recv_sem, slab_send, slab_recv):
    nx, ny, nz = sizes
    _, depth, rows, lanes = field.shape
    total = rows + 2 * EDGE
    ix, iy, iz = (lax.axis_index(name) for name in ("gx", "gy", "gz"))
    spots = {"gx": (ix, nx), "gy": (iy, ny), "gz": (iz, nz)}

    def has(axis, step):
        place, count = spots[axis]
        return place > 0 if step < 0 else place < count - 1

    def target(axis, step):
        return {axis: spots[axis][0] + step}

    barrier = pltpu.get_barrier_semaphore()
    for axis in ("gx", "gy"):
        for step in (-1, 1):
            @pl.when(has(axis, step))
            def _():
                pl.semaphore_signal(barrier, inc=1, device_id=target(axis, step), device_id_type=MESH)
    for j in range(1, nz):
        pl.semaphore_signal(barrier, inc=1, device_id={"gz": lax.rem(iz + j, nz)}, device_id_type=MESH)

    own = pltpu.make_async_copy(
        field, box.at[:, pl.ds(3, depth), pl.ds(EDGE, rows), :], local_sem)
    own.start()

    for step in (-1, 1):
        edge = 0 if step < 0 else EDGE + rows
        @pl.when(jnp.logical_not(has("gx", step)))
        def _():
            box[:, :, edge:edge + EDGE, :] = jnp.zeros((2, depth + 6, EDGE, lanes), jnp.float32)
        first = 0 if step < 0 else depth + 3
        @pl.when(jnp.logical_not(has("gz", step)))
        def _():
            box[:, first:first + 3] = jnp.zeros((2, 3, total, lanes), jnp.float32)
        side = 0 if step < 0 else 1
        @pl.when(jnp.logical_not(has("gy", step)))
        def _():
            got_own[side] = jnp.zeros((2, total, lanes), jnp.float32)
            got_rim[side] = jnp.zeros((total, lanes), jnp.float32)

    azimuth = jnp.full(light.shape[1:], angles[0], jnp.float32)
    polar = jnp.full(light.shape[1:], angles[1], jnp.float32)
    light[0] = jnp.cos(azimuth) * jnp.sin(polar)
    light[1] = jnp.sin(azimuth) * jnp.sin(polar)
    light[2] = jnp.cos(polar)
    for c in range(4):
        line = jnp.broadcast_to(transfer[c:c + 1, :], table.shape[1:])
        table[2 * c] = line
        table[2 * c + 1] = pltpu.roll(line, lanes - 1, 1) - line

    slots = [0]
    links = {}

    def link(name, axis, step, src, dst):
        links[name, step] = (slots[0], axis, step, src, dst)
        slots[0] += 1

    def arrival(name, step):
        slot, axis, _, src, dst = links[name, -step]
        return slot, axis, src, dst

    def copy(name, step):
        slot, axis, _, src, dst = links[name, step]
        return pltpu.make_async_remote_copy(
            src_ref=src, dst_ref=dst, send_sem=send_sem.at[slot], recv_sem=recv_sem.at[slot],
            device_id=target(axis, step), device_id_type=MESH)

    def condition(name, step):
        need = has(links[name, step][1], step)
        return need

    extra = {}

    def begin(name, step):
        need = condition(name, step)
        if name in extra:
            need = jnp.logical_and(need, extra[name])
        @pl.when(need)
        def _():
            copy(name, step).start()

    def sent(name, step):
        need = condition(name, step)
        if name in extra:
            need = jnp.logical_and(need, extra[name])
        @pl.when(need)
        def _():
            copy(name, step).wait_send()

    def got(name, step):
        need = has(links[name, -step][1], step)
        if name in extra:
            need = jnp.logical_and(need, extra[name])
        @pl.when(need)
        def _():
            copy(name, -step).wait_recv()

    every = pl.ds(3, depth)
    middle = pl.ds(EDGE, rows)
    for step in (-1, 1):
        side = 0 if step > 0 else 1
        row = 0 if step < 0 else rows - EDGE
        link("rows", "gx", step, field.at[:, :, pl.ds(row, EDGE), :],
             box.at[:, every, pl.ds(EDGE + rows if step < 0 else 0, EDGE), :])
        plane = 0 if step < 0 else depth - 3
        to = depth + 3 if step < 0 else 0
        link("planes", "gz", step, field.at[:, pl.ds(plane, 3)], box.at[:, pl.ds(to, 3), middle, :])
        for name, at in (("low", 0), ("high", EDGE + rows)):
            link("planes " + name, "gz", step, box.at[:, pl.ds(3 + plane, 3), pl.ds(at, EDGE), :],
                 box.at[:, pl.ds(to, 3), pl.ds(at, EDGE), :])
        for name, at, count in (("middle", EDGE, rows), ("low", 0, EDGE), ("high", EDGE + rows, EDGE)):
            link("strips " + name, "gy", step, own_strips.at[:, pl.ds(at, count), :],
                 got_own.at[side, :, pl.ds(at, count), :])
        link("rims", "gy", step, rim_strips, got_rim.at[side])
    extra["planes low"] = has("gx", -1)
    extra["planes high"] = has("gx", 1)

    count = nz - 1
    for axis in ("gx", "gy"):
        for step in (-1, 1):
            count = count + has(axis, step).astype(jnp.int32)
    pl.semaphore_wait(barrier, count)

    for step in (-1, 1):
        begin("rows", step)
    for step in (-1, 1):
        begin("planes", step)

    lane = lax.broadcasted_iota(jnp.int32, (total, lanes), 1)

    def in_group(lane, group):
        return jnp.bitwise_and(lane + (3 + lanes) - 8 * group, lanes - 1) < 6

    def pack(at, count):
        here = lane[:count]
        def turn(z, kept):
            mask = in_group(here, z)
            return tuple(
                jnp.where(mask, pltpu.roll(box[v, 3 + z, at:at + count, :], 8 * z, 1), kept[v])
                for v in range(2))
        empty = jnp.zeros((count, lanes), jnp.float32)
        first, second = lax.fori_loop(0, depth, turn, (empty, empty))
        own_strips[0, at:at + count, :] = first
        own_strips[1, at:at + count, :] = second

    own.wait()
    pack(EDGE, rows)
    for step in (-1, 1):
        begin("strips middle", step)
    for step, name, at in ((-1, "low", 0), (1, "high", EDGE + rows)):
        got("rows", step)
        for way in (-1, 1):
            begin("planes " + name, way)
        pack(at, EDGE)
        for way in (-1, 1):
            begin("strips " + name, way)

    def merged(left, right):
        here = jnp.bitwise_and(lax.broadcasted_iota(jnp.int32, left.shape, 1), 7)
        return jnp.where(here >= 4, left, right)

    for name in ("middle", "low", "high"):
        for step in (-1, 1):
            got("strips " + name, step)
    for name in ("middle", "low", "high"):
        for step in (-1, 1):
            sent("strips " + name, step)
    for v in range(2):
        own_strips[v] = merged(got_own[0, v], got_own[1, v])

    part = 40 if total % 40 == 0 else EDGE

    def along_y(plane, group_of, strips_of):
        for at in range(0, total, part):
            here = lane[:part]
            for v in range(2):
                block = box[v, plane, at:at + part, :]
                group = group_of(v)
                halo = pltpu.roll(strips_of(v, at, part), lanes - 8 * group, 1)

                def place(o):
                    if o == 0:
                        return block
                    if o > 0:
                        return pltpu.roll(jnp.where(here < o, halo, block), lanes - o, 1)
                    return pltpu.roll(jnp.where(here >= lanes + o, halo, block), -o, 1)

                if v == 0:
                    plain, steep = both_of(place)
                    rows_done[0, plane, at:at + part, :] = plain
                    rows_done[1, plane, at:at + part, :] = steep
                else:
                    rows_done[2, plane, at:at + part, :] = smooth_of(place)

    def along_x(plane):
        width = 32 if rows % 32 == 0 else EDGE
        for at in range(0, rows, width):
            def reader(k):
                return lambda o: rows_done[k, plane, EDGE + at + o:EDGE + at + o + width, :]
            plain, steep = both_of(reader(0))
            flat_done[0, plane, at:at + width, :] = plain
            flat_done[1, plane, at:at + width, :] = steep
            flat_done[2, plane, at:at + width, :] = smooth_of(reader(1))
            flat_done[3, plane, at:at + width, :] = smooth_of(reader(2))

    def own_plane(z, carry):
        along_y(z + 3, lambda v: z, lambda v, at, count: own_strips[v, at:at + count, :])
        return carry

    def own_plane_x(z, carry):
        along_x(z + 3)
        return carry

    lax.fori_loop(0, depth, own_plane, 0)
    lax.fori_loop(0, depth, own_plane_x, 0)

    for step in (-1, 1):
        got("planes", step)
        got("planes low", step)
        got("planes high", step)

    def pack_rim(h, kept):
        plane = jnp.where(h < 3, h, h + depth)
        for v in range(2):
            group = 8 * v + h
            kept = jnp.where(in_group(lane, group), pltpu.roll(box[v, plane], 8 * group, 1), kept)
        return kept

    rim_strips[...] = lax.fori_loop(0, 6, pack_rim, jnp.zeros((total, lanes), jnp.float32))
    for step in (-1, 1):
        begin("rims", step)

    chunk = light.shape[1]

    def sample(z, at):
        def reader(k):
            return lambda o: flat_done[k, z + 3 + o, pl.ds(at, chunk), :]
        value, grad_z = both_of(reader(0))
        grad_x = smooth_of(reader(1))
        grad_y = smooth_of(reader(2))
        mixture = smooth_of(reader(3))
        position = (lanes - 1) / (1.0 + jnp.exp(-value))
        index = jnp.minimum(position.astype(jnp.int32), lanes - 2)
        share = position - index.astype(jnp.float32)

        def look(c):
            low = jnp.take_along_axis(table[2 * c], index, axis=1, mode="promise_in_bounds")
            rise = jnp.take_along_axis(table[2 * c + 1], index, axis=1, mode="promise_in_bounds")
            return low + share * rise

        facing = grad_x * light[0] + grad_y * light[1] + grad_z * light[2]
        square = grad_x * grad_x + grad_y * grad_y + grad_z * grad_z + SHADE_FLOOR
        shade = 0.25 + 0.75 * (facing * facing / square)
        alpha = 1.0 - jnp.exp((-OPTICAL * depth_step) * look(3) / (1.0 + jnp.exp(-mixture)))
        lit = alpha * shade
        return (lit * look(0), lit * look(1), lit * look(2), alpha)

    def over(front, back):
        left = 1.0 - front[3]
        return tuple(f + left * b for f, b in zip(front, back))

    nothing = tuple(jnp.zeros((chunk, lanes), jnp.float32) for _ in range(4))

    def inner_chunk(c, carry):
        at = pl.multiple_of(c * chunk, chunk)
        result = lax.fori_loop(3, depth - 3, lambda z, acc: over(acc, sample(z, at)), nothing)
        for k in range(4):
            inner[k, pl.ds(at, chunk), :] = result[k]
        return carry

    lax.fori_loop(0, rows // chunk, inner_chunk, 0)

    for step in (-1, 1):
        got("rims", step)
    for step in (-1, 1):
        sent("rims", step)
    rim_strips[...] = merged(got_rim[0], got_rim[1])

    def rim_plane(h, carry):
        plane = jnp.where(h < 3, h, h + depth)
        along_y(plane, lambda v: 8 * v + h, lambda v, at, count: rim_strips[at:at + count, :])
        return carry

    def rim_plane_x(h, carry):
        along_x(jnp.where(h < 3, h, h + depth))
        return carry

    lax.fori_loop(0, 6, rim_plane, 0)
    lax.fori_loop(0, 6, rim_plane_x, 0)

    height = rows // nz

    def slab_copy(j):
        return pltpu.make_async_remote_copy(
            src_ref=stage.at[j - 1], dst_ref=slabs.at[iz], send_sem=slab_send.at[j - 1],
            recv_sem=slab_recv.at[iz], device_id={"gz": lax.rem(iz + j, nz)}, device_id_type=MESH)

    for j in range(1, nz + 1):
        slab = lax.rem(iz + j, nz)

        def slab_chunk(c, carry):
            here = pl.multiple_of(c * chunk, chunk)
            at = pl.multiple_of(slab * height + c * chunk, chunk)
            acc = lax.fori_loop(0, 3, lambda z, a: over(a, sample(z, at)), nothing)
            acc = over(acc, tuple(inner[k, pl.ds(at, chunk), :] for k in range(4)))
            acc = lax.fori_loop(depth - 3, depth, lambda z, a: over(a, sample(z, at)), acc)
            for k in range(4):
                if j < nz:
                    stage[j - 1, k, pl.ds(here, chunk), :] = acc[k]
                else:
                    slabs[iz, k, pl.ds(here, chunk), :] = acc[k]
            return carry

        lax.fori_loop(0, height // chunk, slab_chunk, 0)
        if j < nz:
            slab_copy(j).start()

    for j in range(1, nz):
        source = lax.rem(iz + j, nz)
        pltpu.make_async_remote_copy(
            src_ref=stage.at[j - 1], dst_ref=slabs.at[source], send_sem=slab_send.at[j - 1],
            recv_sem=slab_recv.at[source], device_id={"gz": source}, device_id_type=MESH).wait_recv()

    image = tuple(slabs[0, k] for k in range(4))
    for k in range(1, nz):
        image = over(image, tuple(slabs[k, c] for c in range(4)))
    for c in range(4):
        out[c] = image[c]

    for name in ("rows", "planes", "planes low", "planes high"):
        for step in (-1, 1):
            sent(name, step)
    for j in range(1, nz):
        slab_copy(j).wait_send()


def shards(sizes, field, transfer, light_angles):
    nx, ny, nz = sizes
    _, depth, rows, lanes = field.shape
    total = rows + 2 * EDGE
    height = rows // nz
    chunk = min(height, 16)
    full = depth + 6
    f32 = jnp.float32
    return pl.pallas_call(
        functools.partial(kernel, sizes, 1.0 / (depth * nz)),
        out_shape=jax.ShapeDtypeStruct((4, height, lanes), f32),
        in_specs=[
            pl.BlockSpec(memory_space=pl.ANY),
            pl.BlockSpec(memory_space=pltpu.VMEM),
            pl.BlockSpec(memory_space=pltpu.SMEM),
        ],
        out_specs=pl.BlockSpec(memory_space=pltpu.VMEM),
        scratch_shapes=[
            pltpu.VMEM((2, full, total, lanes), f32),
            pltpu.VMEM((2, total, lanes), f32),
            pltpu.VMEM((total, lanes), f32),
            pltpu.VMEM((2, 2, total, lanes), f32),
            pltpu.VMEM((2, total, lanes), f32),
            pltpu.VMEM((3, full, total, lanes), f32),
            pltpu.VMEM((4, full, rows, lanes), f32),
            pltpu.VMEM((8, chunk, lanes), f32),
            pltpu.VMEM((3, chunk, lanes), f32),
            pltpu.VMEM((4, rows, lanes), f32),
            pltpu.VMEM((nz - 1, 4, height, lanes), f32),
            pltpu.VMEM((nz, 4, height, lanes), f32),
            pltpu.SemaphoreType.DMA,
            pltpu.SemaphoreType.DMA((16,)),
            pltpu.SemaphoreType.DMA((16,)),
            pltpu.SemaphoreType.DMA((nz,)),
            pltpu.SemaphoreType.DMA((nz,)),
        ],
        compiler_params=pltpu.CompilerParams(
            collective_id=0, has_side_effects=True, vmem_limit_bytes=40 * 1024 * 1024),
    )(field, transfer, light_angles)


def solution(mesh):
    sizes = tuple(mesh.shape[name] for name in ("gx", "gy", "gz"))
    placed = (P(None, "gz", "gx", "gy"), P(), P())
    return jax.shard_map(
        functools.partial(shards, sizes), mesh=mesh, in_specs=placed,
        out_specs=P(None, ("gx", "gz"), "gy"), check_vma=False
    )
```

time: 152 us -> 33.7 us (0.22); the launches traced: 150 us -> 33.5 us
  other arithmetic: 47.2 us -> 0 us
  matrix products: 45.2 us -> 0 us
  Pallas kernels: 0 us -> 30.3 us
  local copies, waits for them, and re-layouts: 18.6 us -> 3.19 us
  starting transfers between devices: 14.1 us -> 0 us
  waiting for transfers between devices: 14.1 us -> 0 us
  blocking collectives: 5.91 us -> 0 us
  between operations: 3.13 us -> 0.01 us
    dot_general x16 -> x0, matrix products: 45.2 us -> none  [sample_plane(): jnp.einsum('cb,bxy->cxy', transfer, tent, precision=lax.Precision.HIGHEST)]
    pallas_call x0 -> x1, Pallas kernels: none -> 30.3 us  [shards(): pl.pallas_call(functools.partial(kernel, sizes, 1.0 / (depth * nz)), out_...]
    ppermute x6 -> x0, starting transfers between devices: 14.1 us -> none  [the longest x3 10.3 us: extended(): before = lax.ppermute(last, axis, up)]
    ppermute x6 -> x0, waiting for transfers between devices: 14.1 us -> none  [the longest x3 9.53 us: extended(): after = lax.ppermute(initial, axis, down)]
    mul x52 -> x0, other arithmetic: 13.5 us -> none  [the longest x32 13.4 us: sample_plane(): return jnp.concatenate([(alpha * shade)[None] * looked[:3], alpha[None]], 0)]
    sub x18 -> x0, other arithmetic: 12.5 us -> none  [the longest x16 12.5 us: sample_plane(): position[None] - centers[:, None, None]]
    add x27 -> x0, other arithmetic: 11.6 us -> none  [the longest x9 10.2 us: sweep(): total + taps[place] * lax.slice_in_dim(volume, place, place + length, axi...]
    concatenate x2 -> x0, other arithmetic: 7.96 us -> none  [extended(): value = jnp.concatenate([before, value, after], axis=dim)]
  transfers between devices with their start and end apart: 6 -> 0, of which waited for: 4 -> 0; matrix products, arithmetic and copies ran while one was open for 4% -> 0% of each run, Pallas kernels for 0% -> 0%
where the time goes in v1:
time: 33.7 us; the launch traced here: 33.5 us
  Pallas kernels  30.3 us (90%)
  local copies, waits for them, and re-layouts  3.19 us (9%)
    pallas_call x1, Pallas kernels, shards(): pl.pallas_call(functools.partial(kernel, sizes, 1.0 / (depth * nz)), out_...  30.3 us
    unnamed x7, local copies, waits for them, and re-layouts  3.19 us

profile of v1, /device:TPU:0, one launch (start us, length us, event | category | flops | bytes accessed | tf_op | source)
XLA Modules:
  0.0 33.5 jit_solution(8860882351699940247)
XLA Ops:
  0.0 0.0 copy-start
  0.0 1.2 %copy-done = f32[2,16,64,128]{3,2,1,0:T(8,128)S(1)} copy-done((f32[2,16,64,128]{3,2,1,0:T(8,128)S(1)}, f32[2,16,64,128]{3,2,1,0:T(8,128)}, u32[]{:S(2)}) %copy-start) | copy-done | bytes 1048600
  1.2 0.0 copy-start.1
  1.2 0.7 %copy-done.1 = f32[4,128]{1,0:T(4,128)S(1)} copy-done((f32[4,128]{1,0:T(4,128)S(1)}, f32[4,128]{1,0:T(4,128)}, u32[]{:S(2)}) %copy-start.1) | copy-done | bytes 2072
  1.9 0.0 copy-start.2
  1.9 0.7 %copy-done.2 = f32[2]{0:T(128)S(1)} copy-done((f32[2]{0:T(128)S(1)}, f32[2]{0:T(128)}, u32[]{:S(2)}) %copy-start.2) | copy-done | bytes 32
  2.6 30.3 %shard_map.37 = f32[4,32,128]{2,1,0:T(8,128)S(1)} custom-call(f32[2,16,64,128]{3,2,1,0:T(8,128)S(1)} %copy-done, f32[4,128]{1,0:T(4,128)S(1)} %copy-done.1, f32[2]{0:T(128)S(1)} %copy-done.2), custom_call_target="tpu_custom_call" | custom-call | tf_op jit(solution)/shard_map/pallas_call | solution.py:403
  32.9 0.6 %copy.5 = f32[4,32,128]{2,1,0:T(8,128)} copy(f32[4,32,128]{2,1,0:T(8,128)S(1)} %shard_map.37) | data formatting | bytes 131072
Async XLA Ops:
  0.0 1.2 %copy-start = (f32[2,16,64,128]{3,2,1,0:T(8,128)S(1)}, f32[2,16,64,128]{3,2,1,0:T(8,128)}, u32[]{:S(2)}) copy-start(f32[2,16,64,128]{3,2,1,0:T(8,128)} %field.1) | copy-start | bytes 3145732
  1.2 0.7 %copy-start.1 = (f32[4,128]{1,0:T(4,128)S(1)}, f32[4,128]{1,0:T(4,128)}, u32[]{:S(2)}) copy-start(f32[4,128]{1,0:T(4,128)} %transfer.1) | copy-start | bytes 6148
  1.9 0.7 %copy-start.2 = (f32[2]{0:T(128)S(1)}, f32[2]{0:T(128)}, u32[]{:S(2)}) copy-start(f32[2]{0:T(128)} %angles.1) | copy-start | bytes 28
